TPU v7x, 512 devices: a whole 4x8x8 slice. The times are simulated.
512 devices in a mesh: src: 64 (over z, y), tgt: 8 (over x, core).
Axes of the slice: x: 4, y: 8, z: 8, core: 2. Of those that a mesh axis runs over, the one named last changes fastest.
Arguments:
- source_points: float32 [50, 131072], P(None, ('src', 'tgt')), may hold values from -1.8 to 1.8
- source_potential: float32 [131072], P(('src', 'tgt')), may hold values from -4 to 452
- source_logw: float32 [131072], P('src'), may hold values from -2 to 2
- target_points: float32 [50, 131072], P(None, 'tgt'), may hold values from -1.8 to 1.8
- target_logw: float32 [131072], P('tgt'), may hold values from -4 to 452
- pair_source: int32 [64, 8, 256], P('src', 'tgt'), may hold values from 0 to 15, as said below
- pair_target: int32 [64, 8, 256], P('src', 'tgt'), may hold values from 0 to 127
- pair_count: int32 [64, 8], P('src', 'tgt'), may hold values from 128 to 256, as said below
Outputs:
- target_potential: float32 [131072], P('tgt')
- updated_source: float32 [131072], P('src')
Inputs may be any that keep to these rules, and one draw needn't show every extreme that they name: `pair_source`: on each device the pairs in the used slots are distinct; slots 0 to 127 are always used, name every target block of the device exactly once and every source block of the device at least once; unused slots hold numbers in range but are not pairs. `pair_count`: in every draw some device uses all 256 slots and another exactly 128.
All inputs are finite; a program needn't handle non-finite values.
Results may differ from a plain program's by a relative error of at most 0.0003.
Values sent between devices are 32-bit elements; how exact they have to be, the bound alone decides.
A program may use at most 64 MiB of HBM per device.

v0:
```python
import jax
import jax.numpy as jnp
from jax import lax
from jax.sharding import PartitionSpec as P

BLOCK = 128


entropic = 0.5
lowest = -1e30
group_slots = 16


def pick_rows(chosen, rows):
    return jnp.sum(jnp.where(chosen[:, :, None], rows[None, :, :], 0.0), axis=1)


def reduce_pairs(own_pts, own_ids, far_pts, far_vals, far_ids, count, groups):
    width = own_pts.shape[0]
    own_blocks = own_pts.reshape(width, -1, BLOCK)
    far_blocks = far_pts.reshape(width, -1, BLOCK)
    far_rows = far_vals.reshape(-1, BLOCK)
    n_own = own_blocks.shape[1]
    n_far = far_blocks.shape[1]
    own_sq = jnp.sum(own_blocks * own_blocks, axis=0)
    far_sq = jnp.sum(far_blocks * far_blocks, axis=0)
    owners = jnp.arange(n_own, dtype=jnp.int32)
    others = jnp.arange(n_far, dtype=jnp.int32)

    def step(k, carry):
        peak, total = carry
        start = (k * group_slots).astype(jnp.int32)
        own_g = lax.dynamic_slice_in_dim(own_ids, start, group_slots)
        far_g = lax.dynamic_slice_in_dim(far_ids, start, group_slots)
        valid = start + jnp.arange(group_slots, dtype=jnp.int32) < count
        own_hit = own_g[:, None] == owners[None, :]
        far_hit = far_g[:, None] == others[None, :]
        own_sel = jnp.einsum(
            "gn,cnb->cgb", own_hit.astype(jnp.float32), own_blocks, precision=lax.Precision.HIGHEST
        )
        far_sel = jnp.einsum(
            "gn,cnb->cgb", far_hit.astype(jnp.float32), far_blocks, precision=lax.Precision.HIGHEST
        )
        cross = jnp.einsum("cga,cgb->gab", far_sel, own_sel, precision=lax.Precision.HIGHEST)
        cost = (
            pick_rows(far_hit, far_sq)[:, :, None]
            + pick_rows(own_hit, own_sq)[:, None, :]
            - 2.0 * cross
        )
        score = (pick_rows(far_hit, far_rows)[:, :, None] - cost) / entropic
        tile_peak = jnp.max(score, axis=1)
        tile_total = jnp.sum(jnp.exp(score - tile_peak[:, None, :]), axis=1)
        tile_peak = jnp.where(valid[:, None], tile_peak, lowest)
        tile_total = jnp.where(valid[:, None], tile_total, 0.0)
        match = own_hit & valid[:, None]
        spread = jnp.where(match[:, :, None], tile_peak[:, None, :], lowest)
        new_peak = jnp.maximum(peak, jnp.max(spread, axis=0))
        own_peak = jnp.max(jnp.where(own_hit[:, :, None], new_peak[None, :, :], lowest), axis=1)
        lifted = tile_total * jnp.exp(tile_peak - own_peak)
        added = jnp.dot(match.T.astype(jnp.float32), lifted, precision=lax.Precision.HIGHEST)
        return (new_peak, total * jnp.exp(peak - new_peak) + added)

    peak0 = jnp.full((n_own, BLOCK), lowest, jnp.float32)
    total0 = jnp.zeros((n_own, BLOCK), jnp.float32)
    return lax.fori_loop(0, groups, step, (peak0, total0))


def local(
    source_points,
    source_potential,
    source_logw,
    target_points,
    target_logw,
    pair_source,
    pair_target,
    pair_count,
):
    points, potential = (
        lax.all_gather(source_points, "tgt", axis=1, tiled=True),
        lax.all_gather(source_potential, "tgt", axis=0, tiled=True),
    )
    ids_src = pair_source.reshape(-1)
    ids_tgt = pair_target.reshape(-1)
    count = pair_count.reshape(())
    slots = ids_src.shape[0]
    groups = slots // group_slots
    peak, total = reduce_pairs(target_points, ids_tgt, points, potential, ids_src, count, groups)
    top = lax.pmax(peak, "src")
    scaled = total * jnp.exp(peak - top)
    summed = lax.psum(scaled, "src")
    target_potential = entropic * target_logw - entropic * (top + jnp.log(summed)).reshape(-1)
    row_peak, row_sum = reduce_pairs(
        points, ids_src, target_points, target_potential, ids_tgt, count, groups
    )
    top_row = lax.pmax(row_peak, "tgt")
    summed_row = lax.psum(row_sum * jnp.exp(row_peak - top_row), "tgt")
    updated_source = entropic * source_logw - entropic * (top_row + jnp.log(summed_row)).reshape(-1)
    return (target_potential, updated_source)


def solution(mesh):
    placed = (
        P(None, ("src", "tgt")),
        P(("src", "tgt")),
        P("src"),
        P(None, "tgt"),
        P("tgt"),
        P("src", "tgt", None),
        P("src", "tgt", None),
        P("src", "tgt"),
    )
    return jax.shard_map(
        local, mesh=mesh, in_specs=placed, out_specs=(P("tgt"), P("src")), check_vma=False
    )
```

profile of v0, /device:TPU:1, one launch (start us, length us, event | category | flops | bytes accessed | tf_op | source)
XLA Modules:
  0.0 696.2 jit_solution(2597616311463734729)
XLA Ops:
  7.2 20.1 %all_gather.7 = f32[50,2048]{1,0:T(8,128)S(1)} all-gather(f32[50,256]{1,0:T(8,128)} %param.12), channel_id=1, replica_groups=mesh['src'=64,'tgt'=8] {'tgt'}, dimensions={1}, use_global_device_ids=true | all-gather | bytes 460800 | tf_op jit(solution)/shard_map/all_gather | solution.py:79
  28.3 2.4 multiply_reduce_fusion
  32.0 8.9 %all-gather = f32[8,1,256]{2,1,0:T(1,128)} all-gather(f32[1,1,256]{2,1,0:T(1,128)S(1)} %bitcast.78), channel_id=1, replica_groups=mesh['src'=64,'tgt'=8] {'tgt'}, dimensions={0}, use_global_device_ids=true | all-gather | bytes 9216 | tf_op jit(solution)/shard_map/all_gather | solution.py:80
  40.9 184.2 %while.32 = (s32[]{:T(128)}, f32[128,128]{1,0:T(8,128)S(1)}, f32[128,128]{1,0:T(8,128)S(1)}, s32[256]{0:T(256)}, s32[]{:T(128)}, /*index=5*/s32[256]{0:T(256)}, ...) while((s32[]{:T(128)}, f32[128,128]{1,0:T(8,128)S(1)}, ...), condition=%wide.region_10.11_spmd.clone, body=%wide.region_2.10_spmd.clone.sunk | while | flops 341029536 | bytes 12095238 | solution.py:65
  44.0 1.9 convolution_multiply_fusion.3
  47.6 1.8 fusion.88
  49.8 1.5 select_reduce_fusion.19
  55.5 1.9 convolution_multiply_fusion.3
  59.1 1.8 fusion.88
  61.3 1.5 select_reduce_fusion.19
  67.0 1.9 convolution_multiply_fusion.3
  70.6 1.8 fusion.88
  72.8 1.5 select_reduce_fusion.19
  78.6 1.9 convolution_multiply_fusion.3
  82.1 1.8 fusion.88
  84.4 1.5 select_reduce_fusion.19
  90.1 1.9 convolution_multiply_fusion.3
  93.6 1.8 fusion.88
  95.9 1.5 select_reduce_fusion.19
  101.6 1.9 convolution_multiply_fusion.3
  105.1 1.8 fusion.88
  107.4 1.5 select_reduce_fusion.19
  113.1 1.9 convolution_multiply_fusion.3
  116.7 1.8 fusion.88
  124.6 1.9 convolution_multiply_fusion.3
  128.2 1.8 fusion.88
  130.4 1.5 select_reduce_fusion.19
  136.1 1.9 convolution_multiply_fusion.3
  139.7 1.8 fusion.88
  147.7 1.9 convolution_multiply_fusion.3
  151.2 1.8 fusion.88
  159.2 1.9 convolution_multiply_fusion.3
  162.7 1.8 fusion.88
  170.7 1.9 convolution_multiply_fusion.3
  174.2 1.8 fusion.88
  182.2 1.9 convolution_multiply_fusion.3
  185.7 1.8 fusion.88
  193.7 1.9 convolution_multiply_fusion.3
  197.3 1.8 fusion.88
  205.2 1.9 convolution_multiply_fusion.3
  208.8 1.8 fusion.88
  216.7 1.9 convolution_multiply_fusion.3
  220.3 1.8 fusion.88
  225.8 143.6 %all-reduce.3.cloned.1.call-done = f32[128,128]{1,0:T(8,128)} async-done(((f32[128,128]{1,0:T(8,128)}), f32[128,128]{1,0:T(8,128)}) %all-reduce.3.cloned.1.call-update) | async-done | bytes 65552 | tf_op jit(solution)/shard_map/pmax | solution.py:88
  371.0 146.6 %all-reduce.5.cloned.1.call-done = f32[128,128]{1,0:T(8,128)} async-done(((f32[128,128]{1,0:T(8,128)}), f32[128,128]{1,0:T(8,128)}) %all-reduce.5.cloned.1.call-update) | async-done | bytes 65552 | tf_op jit(solution)/shard_map/psum | solution.py:90
  518.6 140.2 %while.33 = (s32[]{:T(128)}, f32[16,128]{1,0:T(8,128)S(1)}, f32[16,128]{1,0:T(8,128)S(1)}, s32[256]{0:T(256)}, s32[]{:T(128)}, /*index=5*/s32[256]{0:T(256)}, f3...) while((s32[]{:T(128)}, f32[16,128]{1,0:T(8,128)S(1)}, ...), condition=%wide.region_21.22_spmd.clone, body=%wide.region_13.21_spmd.clone.sunk | while | flops 337984800 | bytes 7788630 | solution.py:65
  523.9 2.6 fusion.96
  532.7 2.6 fusion.96
  541.5 2.6 fusion.96
  550.2 2.6 fusion.96
  559.0 2.6 fusion.96
  567.8 2.6 fusion.96
  576.5 2.6 fusion.96
  585.3 2.6 fusion.96
  594.1 2.6 fusion.96
  602.8 2.6 fusion.96
  611.6 2.6 fusion.96
  620.3 2.6 fusion.96
  629.1 2.6 fusion.96
  637.9 2.6 fusion.96
  646.6 2.6 fusion.96
  655.4 2.6 fusion.96
  658.8 17.3 %pmax.15 = f32[16,128]{1,0:T(8,128)S(1)} all-reduce(f32[16,128]{1,0:T(8,128)S(1)} %get-tuple-element.434), channel_id=1, replica_groups=mesh['src'=64,'tgt'=8] {'tgt'}, use_global_device_ids=true, to_apply=%region_22.23 | all-reduce | flops 2048 | bytes 16384 | tf_op jit(solution)/shard_map/pmax | solution.py:95
  676.1 12.7 %psum.15 = f32[16,128]{1,0:T(8,128)S(1)} all-reduce(f32[16,128]{1,0:T(8,128)S(1)} %exponential_multiply_fusion.1), channel_id=1, replica_groups=mesh['src'=64,'tgt'=8] {'tgt'}, use_global_device_ids=true, to_apply=%region_23.24 | all-reduce | flops 2048 | bytes 16384 | tf_op jit(solution)/shard_map/psum | solution.py:96
  (628 shorter events, 215.9 us)
Async XLA Ops:
  7.2 362.3 %all-reduce.3.cloned.1.call-start = ((), (), s32[]{:S(2)}) async-start(), calls=%async_computation | async-start | bytes 131072 | tf_op jit(solution)/shard_map/pmax | solution.py:88
  7.2 23.5 %copy-start.1 = (f32[50,16384]{1,0:T(8,128)S(1)}, f32[50,16384]{1,0:T(8,128)}, u32[]{:S(2)}) copy-start(f32[50,16384]{1,0:T(8,128)} %param.15) | copy-start | bytes 9830404
  41.7 7.7 %copy-start.6 = (s32[16]{0:T(128)}, s32[16]{0:T(128)S(1)}, u32[]{:S(2)}) copy-start(s32[16]{0:T(128)S(1)} %dynamic_slice.36) | copy-start | bytes 196 | tf_op jit(solution)/shard_map/while
  46.6 2.9 copy-start.5
  46.6 2.8 copy-start.4
  52.4 2.7 copy-start
  53.2 7.7 %copy-start.6 = (s32[16]{0:T(128)}, s32[16]{0:T(128)S(1)}, u32[]{:S(2)}) copy-start(s32[16]{0:T(128)S(1)} %dynamic_slice.36) | copy-start | bytes 196 | tf_op jit(solution)/shard_map/while
  58.1 2.9 copy-start.5
  58.2 2.8 copy-start.4
  63.9 2.7 copy-start
  64.7 7.7 %copy-start.6 = (s32[16]{0:T(128)}, s32[16]{0:T(128)S(1)}, u32[]{:S(2)}) copy-start(s32[16]{0:T(128)S(1)} %dynamic_slice.36) | copy-start | bytes 196 | tf_op jit(solution)/shard_map/while
  69.6 2.9 copy-start.5
  69.7 2.8 copy-start.4
  75.4 2.7 copy-start
  76.3 7.7 %copy-start.6 = (s32[16]{0:T(128)}, s32[16]{0:T(128)S(1)}, u32[]{:S(2)}) copy-start(s32[16]{0:T(128)S(1)} %dynamic_slice.36) | copy-start | bytes 196 | tf_op jit(solution)/shard_map/while
  81.1 2.9 copy-start.5
  81.2 2.8 copy-start.4
  87.0 2.7 copy-start
  87.8 7.7 %copy-start.6 = (s32[16]{0:T(128)}, s32[16]{0:T(128)S(1)}, u32[]{:S(2)}) copy-start(s32[16]{0:T(128)S(1)} %dynamic_slice.36) | copy-start | bytes 196 | tf_op jit(solution)/shard_map/while
  92.6 2.9 copy-start.5
  92.7 2.8 copy-start.4
  98.5 2.7 copy-start
  99.3 7.7 %copy-start.6 = (s32[16]{0:T(128)}, s32[16]{0:T(128)S(1)}, u32[]{:S(2)}) copy-start(s32[16]{0:T(128)S(1)} %dynamic_slice.36) | copy-start | bytes 196 | tf_op jit(solution)/shard_map/while
  104.1 2.9 copy-start.5
  104.2 2.8 copy-start.4
  110.0 2.7 copy-start
  110.8 7.7 %copy-start.6 = (s32[16]{0:T(128)}, s32[16]{0:T(128)S(1)}, u32[]{:S(2)}) copy-start(s32[16]{0:T(128)S(1)} %dynamic_slice.36) | copy-start | bytes 196 | tf_op jit(solution)/shard_map/while
  115.7 2.9 copy-start.5
  115.7 2.8 copy-start.4
  121.5 2.7 copy-start
  122.3 7.7 %copy-start.6 = (s32[16]{0:T(128)}, s32[16]{0:T(128)S(1)}, u32[]{:S(2)}) copy-start(s32[16]{0:T(128)S(1)} %dynamic_slice.36) | copy-start | bytes 196 | tf_op jit(solution)/shard_map/while
  127.2 2.9 copy-start.5
  127.3 2.8 copy-start.4
  133.0 2.7 copy-start
  133.8 7.7 %copy-start.6 = (s32[16]{0:T(128)}, s32[16]{0:T(128)S(1)}, u32[]{:S(2)}) copy-start(s32[16]{0:T(128)S(1)} %dynamic_slice.36) | copy-start | bytes 196 | tf_op jit(solution)/shard_map/while
  138.7 2.9 copy-start.5
  138.8 2.8 copy-start.4
  144.5 2.7 copy-start
  145.3 7.7 %copy-start.6 = (s32[16]{0:T(128)}, s32[16]{0:T(128)S(1)}, u32[]{:S(2)}) copy-start(s32[16]{0:T(128)S(1)} %dynamic_slice.36) | copy-start | bytes 196 | tf_op jit(solution)/shard_map/while
  150.2 2.9 copy-start.5
  150.3 2.8 copy-start.4
  156.0 2.7 copy-start
  156.9 7.7 %copy-start.6 = (s32[16]{0:T(128)}, s32[16]{0:T(128)S(1)}, u32[]{:S(2)}) copy-start(s32[16]{0:T(128)S(1)} %dynamic_slice.36) | copy-start | bytes 196 | tf_op jit(solution)/shard_map/while
  161.7 2.9 copy-start.5
  161.8 2.8 copy-start.4
  168.4 7.7 %copy-start.6 = (s32[16]{0:T(128)}, s32[16]{0:T(128)S(1)}, u32[]{:S(2)}) copy-start(s32[16]{0:T(128)S(1)} %dynamic_slice.36) | copy-start | bytes 196 | tf_op jit(solution)/shard_map/while
  173.2 2.9 copy-start.5
  173.3 2.8 copy-start.4
  179.9 7.7 %copy-start.6 = (s32[16]{0:T(128)}, s32[16]{0:T(128)S(1)}, u32[]{:S(2)}) copy-start(s32[16]{0:T(128)S(1)} %dynamic_slice.36) | copy-start | bytes 196 | tf_op jit(solution)/shard_map/while
  184.7 2.9 copy-start.5
  184.8 2.8 copy-start.4
  191.4 7.7 %copy-start.6 = (s32[16]{0:T(128)}, s32[16]{0:T(128)S(1)}, u32[]{:S(2)}) copy-start(s32[16]{0:T(128)S(1)} %dynamic_slice.36) | copy-start | bytes 196 | tf_op jit(solution)/shard_map/while
  196.3 2.9 copy-start.5
  196.4 2.8 copy-start.4
  202.1 2.7 copy-start
  202.9 7.7 %copy-start.6 = (s32[16]{0:T(128)}, s32[16]{0:T(128)S(1)}, u32[]{:S(2)}) copy-start(s32[16]{0:T(128)S(1)} %dynamic_slice.36) | copy-start | bytes 196 | tf_op jit(solution)/shard_map/while
  207.8 2.9 copy-start.5
  207.9 2.8 copy-start.4
  214.4 7.7 %copy-start.6 = (s32[16]{0:T(128)}, s32[16]{0:T(128)S(1)}, u32[]{:S(2)}) copy-start(s32[16]{0:T(128)S(1)} %dynamic_slice.36) | copy-start | bytes 196 | tf_op jit(solution)/shard_map/while
  219.3 2.9 copy-start.5
  219.4 2.8 copy-start.4
  225.8 291.8 %all-reduce.5.cloned.1.call-start = ((), (), s32[]{:S(2)}) async-start(), calls=%async_computation.1 | async-start | bytes 131072 | tf_op jit(solution)/shard_map/psum | solution.py:90
  518.5 170.2 %copy-start.7 = (f32[2048]{0:T(1024)S(1)}, f32[2048]{0:T(1024)}, u32[]{:S(2)}) copy-start(f32[2048]{0:T(1024)} %param.14) | copy-start | bytes 24580
  658.8 30.6 %copy-start.3 = (f32[16384]{0:T(1024)}, f32[16384]{0:T(1024)S(1)}, u32[]{:S(2)}) copy-start(f32[16384]{0:T(1024)S(1)} %get-tuple-element.833) | copy-start | bytes 196612
  (7 other events, 15.0 us)
Sparse Core Ops, SparseCore 0:
  225.9 143.4 all-reduce.2
  373.6 144.0 all-reduce.4
where the time goes:
time: 700 us; the launch traced here: 696 us
  waiting for transfers between devices  290 us (41%)
  matrix products  158 us (23%)
  other arithmetic  119 us (17%)
  blocking collectives  58.9 us (8%)
  local copies, waits for them, and re-layouts  52.4 us (7%)
  between operations  14.2 us (2%)
    psum x1, waiting for transfers between devices, local(): summed = lax.psum(scaled, 'src')  147 us
    pmax x1, waiting for transfers between devices, local(): top = lax.pmax(peak, 'src')  144 us
    dot_general x32, matrix products, step(): jnp.einsum('cga,cgb->gab', far_sel, own_sel, precision=lax.Precision.HIGH...  72.2 us
    dot_general x32, matrix products, step(): jnp.einsum('gn,cnb->cgb', own_hit.astype(jnp.float32), own_blocks, precis...  40.7 us
    add x16, other arithmetic, step(): pick_rows(far_hit, far_sq)[:, :, None]  28.8 us
    reduce_max x32, other arithmetic, step(): jnp.max(jnp.where(own_hit[:, :, None], new_peak[None, :, :], lowest), axi...  26.3 us
    dynamic_slice x32, local copies, waits for them, and re-layouts, step(): own_g = lax.dynamic_slice_in_dim(own_ids, start, group_slots)  25 us
    dot_general x32, matrix products, step(): jnp.einsum('gn,cnb->cgb', far_hit.astype(jnp.float32), far_blocks, precis...  24.7 us
  transfers between devices with their start and end apart: 2, of which 2 were waited for; matrix products, arithmetic and copies ran while one was open for 0% of the time, Pallas kernels for 0%

commit v1 on v0

v1 whole, which is shorter than its diff:
```python
import functools
import math

import jax
import jax.numpy as jnp
from jax import lax
from jax.experimental import pallas as pl
from jax.experimental.pallas import tpu as pltpu
from jax.sharding import PartitionSpec as P

BLOCK = 128
HALF = 64
ROW_U = 50
ROW_F = 54
LOG2E = 1.4426950408889634
LN2 = 0.6931471805599453
SCALE = 2.0 * LOG2E
ROOT = math.sqrt(2.0 * SCALE)
LOWEST = -1.0e30
UNROLL = 16
CHUNKS = 4
MESH = pl.DeviceIdType.MESH
f32 = jnp.float32
bf16 = jnp.bfloat16


def split(x):
    high = x.astype(bf16)
    return high, (x - high.astype(f32)).astype(bf16)


def residue(x):
    high, low = split(x)
    return x - high.astype(f32) - low.astype(f32)


def rows_of(value, shape):
    return jnp.broadcast_to(value, shape)


def merge(parts):
    top = jnp.max(parts, axis=0)
    return top + jnp.log2(jnp.sum(jnp.exp2(parts - top[None]), axis=0))


def pair_pass(slots, count, left_ids, right_ids, left, right, lse):
    def body(k, carry):
        for step in range(UNROLL):
            p = k * UNROLL + step
            a = left[left_ids[p]]
            r = right[right_ids[p]]
            lhs = jnp.concatenate([a, a], axis=1)
            rhs = jnp.concatenate([r[:HALF], r[:HALF], r[HALF:], r[HALF:]], axis=0)
            score = jnp.dot(lhs, rhs, preferred_element_type=f32)
            top = jnp.max(score, axis=0, keepdims=True)
            total = jnp.sum(jnp.exp2(score - top), axis=0, keepdims=True)
            lse[pl.ds(p, 1), :] = jnp.where(p < count, top + jnp.log2(total), LOWEST)
        return carry

    lax.fori_loop(0, slots // UNROLL, body, 0)


def owner_pass(owners, slots, ids, id_row, lse, peak, scaled):
    index = lax.broadcasted_iota(jnp.int32, (owners, BLOCK), 0)

    def lift(k, top):
        for step in range(8):
            p = k * 8 + step
            row = rows_of(lse[pl.ds(p, 1), :], (owners, BLOCK))
            top = jnp.maximum(top, jnp.where(index == ids[p], row, LOWEST))
        return top

    top = lax.fori_loop(0, slots // 8, lift, jnp.full((owners, BLOCK), LOWEST, f32))
    peak[0:owners, :] = top

    def scale(k, carry):
        tops = jnp.concatenate([peak[pl.ds(ids[k * 8 + step], 1), :] for step in range(8)], axis=0)
        rows = pl.ds(pl.multiple_of(k * 8, 8), 8)
        scaled[rows, :] = jnp.exp2(lse[rows, :] - tops)
        return carry

    lax.fori_loop(0, slots // 8, scale, 0)
    hit = lax.broadcasted_iota(jnp.int32, (owners, slots), 0) == id_row[...]
    pick = jnp.where(hit, 1.0, 0.0).astype(bf16)
    high, low = split(scaled[...])
    total = jnp.dot(pick, high, preferred_element_type=f32) + jnp.dot(
        pick, low, preferred_element_type=f32
    )
    return top + jnp.log2(total)


def kernel(
    dims,
    ids_src, ids_tgt, count_ref,
    row_src, row_tgt, spts, spot, slogw, tlogw, tpts_hbm,
    out_t, out_s,
    tpts, xbuf, r_tgt, a_tgt, r_src, a_src, y_sq, lse, peak, scaled,
    part, recv_y, comb, recv_z, full, rowpart, recv_x,
    load_sem, gather_send, gather_recv, y_send, y_recv, z_send, z_recv, g_send, g_recv, x_send, x_recv,
):
    ny, nz, nt, n_tb, n_sb, slots, pc = dims
    me_s, me_t = lax.axis_index("src"), lax.axis_index("tgt")
    my_y, my_z = lax.rem(me_s, ny), lax.div(me_s, ny)
    per_y = n_tb // ny
    shard_blocks = n_sb // nt
    count = count_ref[0]

    def along_y(d):
        return (my_z * ny + lax.rem(my_y + d, ny), me_t)

    def along_z(d):
        return (lax.rem(my_z + d, nz) * ny + my_y, me_t)

    def along_t(d):
        return (me_s, lax.rem(me_t + d, nt))

    barrier = pltpu.get_barrier_semaphore()
    peers = (
        [along_t(d) for d in range(1, nt)]
        + [along_y(d) for d in range(1, ny)]
        + [along_z(d) for d in range(1, nz)]
    )
    for peer in peers:
        pl.semaphore_signal(barrier, inc=1, device_id=peer, device_id_type=MESH)

    width = n_tb * BLOCK // CHUNKS
    loads = []
    for c in range(CHUNKS):
        cols = pl.ds(c * width, width)
        load = pltpu.make_async_copy(tpts_hbm.at[:, cols], tpts.at[:, cols], load_sem.at[c])
        load.start()
        loads.append(load)

    x = spts[...] * ROOT
    pot = spot[...]
    cells = pot.shape[1]
    u = SCALE * pot - 0.5 * jnp.sum(x * x, axis=0, keepdims=True)
    one = jnp.ones((1, cells), f32)
    xbuf[me_t] = jnp.concatenate([x, u, residue(u), one, one, pot, 0.0 * one], axis=0)

    pl.semaphore_wait(barrier, len(peers))

    def exchange(n, me, where, src, dst, send, recv):
        sent = []
        for d in range(1, n):
            copy = pltpu.make_async_remote_copy(
                src_ref=src(lax.rem(me + d, n)),
                dst_ref=dst(me),
                send_sem=send.at[d - 1],
                recv_sem=recv.at[me],
                device_id=where(d),
                device_id_type=MESH,
            )
            copy.start()
            sent.append(copy)
        return sent

    def collect(n, me, where, dst, send, recv):
        for d in range(1, n):
            other = lax.rem(me + d, n)
            pltpu.make_async_remote_copy(
                src_ref=dst(other),
                dst_ref=dst(other),
                send_sem=send.at[d - 1],
                recv_sem=recv.at[other],
                device_id=where(d),
                device_id_type=MESH,
            ).wait_recv()

    xslot = lambda t: xbuf.at[t]
    sent_g = exchange(nt, me_t, along_t, lambda t: xbuf.at[me_t], xslot, gather_send, gather_recv)

    tail = lax.broadcasted_iota(jnp.int32, (HALF - pc, BLOCK), 0)
    tail = jnp.where(tail < 2, 1.0, 0.0)

    def prepare(k, carry):
        for step in range(4):
            b = k * 4 + step
            y = tpts[:, pl.ds(pl.multiple_of(b * BLOCK, BLOCK), BLOCK)] * ROOT
            y_sq[pl.ds(b, 1), :] = 0.5 * jnp.sum(y * y, axis=0, keepdims=True)
            high, low = split(jnp.concatenate([y, tail], axis=0))
            r_tgt[b] = jnp.concatenate([high, low], axis=0)
        return carry

    per_chunk = n_tb // CHUNKS // 4
    for c in range(CHUNKS):
        loads[c].wait()
        lax.fori_loop(c * per_chunk, (c + 1) * per_chunk, prepare, 0)

    collect(nt, me_t, along_t, xslot, gather_send, gather_recv)
    zeros = jnp.zeros((HALF - 56, BLOCK), f32)
    for t in range(nt):
        for h in range(shard_blocks):
            b = t * shard_blocks + h
            xs = xbuf[t, :, h * BLOCK : (h + 1) * BLOCK]
            high, low = split(jnp.concatenate([xs, zeros], axis=0))
            both = jnp.concatenate([high, low], axis=0)
            r_src[b] = both
            a_src[b] = both.T

    pair_pass(slots, count, ids_src, ids_tgt, a_src, r_tgt, lse)
    part[...] = owner_pass(n_tb, slots, ids_tgt, row_tgt, lse, peak, scaled)

    band = lambda y: pl.ds(pl.multiple_of(y * per_y, per_y), per_y)
    yslot = lambda y: recv_y.at[y]
    sent_y = exchange(ny, my_y, along_y, lambda y: part.at[band(y)], yslot, y_send, y_recv)
    recv_y[my_y] = part[band(my_y), :]
    collect(ny, my_y, along_y, yslot, y_send, y_recv)
    comb[...] = merge(recv_y[...])
    zslot = lambda z: recv_z.at[z]
    sent_z = exchange(nz, my_z, along_z, lambda z: comb, zslot, z_send, z_recv)
    recv_z[my_z] = comb[...]
    collect(nz, my_z, along_z, zslot, z_send, z_recv)
    full[band(my_y), :] = merge(recv_z[...])
    gslot = lambda y: full.at[band(y)]
    sent_a = exchange(ny, my_y, along_y, lambda y: full.at[band(my_y)], gslot, g_send, g_recv)
    collect(ny, my_y, along_y, gslot, g_send, g_recv)

    total = full[...]
    out_t[...] = 0.5 * tlogw[...] - (0.5 * LN2) * (total - y_sq[...])
    peak[...] = LOG2E * tlogw[...] - total

    line = lax.broadcasted_iota(jnp.int32, (16, BLOCK), 0)

    def turn(k, carry):
        for step in range(4):
            b = k * 4 + step
            v = peak[pl.ds(b, 1), :]
            v_high, v_low = split(v)
            rest = residue(v)
            r = r_tgt[b]
            high = r[48:64].astype(f32)
            high = jnp.where(line == 4, v_high.astype(f32), jnp.where(line == 5, rest, high))
            low = jnp.where(line == 4, v_low.astype(f32), r[112:128].astype(f32))
            both = jnp.concatenate([r[:48], high.astype(bf16), r[64:112], low.astype(bf16)], axis=0)
            a_tgt[b] = both.T
        return carry

    lax.fori_loop(0, n_tb // 4, turn, 0)

    pair_pass(slots, count, ids_tgt, ids_src, a_tgt, r_src, lse)
    rowpart[...] = owner_pass(n_sb, slots, ids_src, row_src, lse, peak, scaled)
    rslot = lambda t: recv_x.at[t]
    sent_x = exchange(nt, me_t, along_t, lambda t: rowpart, rslot, x_send, x_recv)
    recv_x[me_t] = rowpart[...]
    collect(nt, me_t, along_t, rslot, x_send, x_recv)
    result = merge(recv_x[...])
    potential = jnp.concatenate(
        [
            xbuf[t, ROW_F : ROW_F + 1, h * BLOCK : (h + 1) * BLOCK]
            for t in range(nt)
            for h in range(shard_blocks)
        ],
        axis=0,
    )
    out_s[...] = potential + 0.5 * slogw[...] - (0.5 * LN2) * result
    for copy in sent_g + sent_y + sent_z + sent_a + sent_x:
        copy.wait_send()


def local(
    n_src,
    n_tgt,
    source_points,
    source_potential,
    source_logw,
    target_points,
    target_logw,
    pair_source,
    pair_target,
    pair_count,
):
    pc, cells = source_points.shape
    n_tb = target_points.shape[1] // BLOCK
    n_sb = source_logw.shape[0] // BLOCK
    slots = pair_source.shape[-1]
    ny = math.isqrt(n_src)
    nz = n_src // ny
    nt = n_tgt
    per_y = n_tb // ny
    vmem = pl.BlockSpec(memory_space=pltpu.VMEM)
    smem = pl.BlockSpec(memory_space=pltpu.SMEM)
    dma = pltpu.SemaphoreType.DMA
    ids_src, ids_tgt = pair_source.reshape(-1), pair_target.reshape(-1)
    out_t, out_s = pl.pallas_call(
        functools.partial(kernel, (ny, nz, nt, n_tb, n_sb, slots, pc)),
        out_shape=(
            jax.ShapeDtypeStruct((n_tb, BLOCK), f32),
            jax.ShapeDtypeStruct((n_sb, BLOCK), f32),
        ),
        in_specs=[smem] * 3 + [vmem] * 6 + [pl.BlockSpec(memory_space=pl.ANY)],
        out_specs=(vmem, vmem),
        scratch_shapes=[
            pltpu.VMEM((pc, n_tb * BLOCK), f32),
            pltpu.VMEM((nt, 56, cells), f32),
            pltpu.VMEM((n_tb, BLOCK, BLOCK), bf16),
            pltpu.VMEM((n_tb, BLOCK, BLOCK), bf16),
            pltpu.VMEM((n_sb, BLOCK, BLOCK), bf16),
            pltpu.VMEM((n_sb, BLOCK, BLOCK), bf16),
            pltpu.VMEM((n_tb, BLOCK), f32),
            pltpu.VMEM((slots, BLOCK), f32),
            pltpu.VMEM((n_tb, BLOCK), f32),
            pltpu.VMEM((slots, BLOCK), f32),
            pltpu.VMEM((n_tb, BLOCK), f32),
            pltpu.VMEM((ny, per_y, BLOCK), f32),
            pltpu.VMEM((per_y, BLOCK), f32),
            pltpu.VMEM((nz, per_y, BLOCK), f32),
            pltpu.VMEM((n_tb, BLOCK), f32),
            pltpu.VMEM((n_sb, BLOCK), f32),
            pltpu.VMEM((nt, n_sb, BLOCK), f32),
            dma((CHUNKS,)),
            dma((nt,)), dma((nt,)),
            dma((ny,)), dma((ny,)),
            dma((nz,)), dma((nz,)),
            dma((ny,)), dma((ny,)),
            dma((nt,)), dma((nt,)),
        ],
        compiler_params=pltpu.CompilerParams(
            collective_id=0, has_side_effects=True, vmem_limit_bytes=40 * 2**20
        ),
    )(
        ids_src,
        ids_tgt,
        pair_count.reshape(-1),
        ids_src.reshape(1, slots),
        ids_tgt.reshape(1, slots),
        source_points,
        source_potential.reshape(1, cells),
        source_logw.reshape(n_sb, BLOCK),
        target_logw.reshape(n_tb, BLOCK),
        target_points,
    )
    return out_t.reshape(-1), out_s.reshape(-1)


def solution(mesh):
    placed = (
        P(None, ("src", "tgt")),
        P(("src", "tgt")),
        P("src"),
        P(None, "tgt"),
        P("tgt"),
        P("src", "tgt", None),
        P("src", "tgt", None),
        P("src", "tgt"),
    )
    return jax.shard_map(
        functools.partial(local, mesh.shape["src"], mesh.shape["tgt"]),
        mesh=mesh,
        in_specs=placed,
        out_specs=(P("tgt"), P("src")),
        check_vma=False,
    )
```

time: 700 us -> 73.4 us (0.10)
  waiting for transfers between devices: 290 us -> 0 us
  matrix products: 158 us -> 0 us
  other arithmetic: 119 us -> 0 us
  Pallas kernels: 0 us -> 64.1 us
  blocking collectives: 58.9 us -> 0 us
  local copies, waits for them, and re-layouts: 52.4 us -> 7.65 us
  between operations: 14.2 us -> 1.3 us
    dot_general x128 -> x0, matrix products: 158 us -> none  [the longest x32 72.2 us: step(): jnp.einsum('cga,cgb->gab', far_sel, own_sel, precision=lax.Precision.HIGH...]
    psum x1 -> x0, waiting for transfers between devices: 147 us -> none  [local(): summed = lax.psum(scaled, 'src')]
    pmax x1 -> x0, waiting for transfers between devices: 144 us -> none  [local(): top = lax.pmax(peak, 'src')]
    pallas_call x0 -> x1, Pallas kernels: none -> 64.1 us  [local(): pl.pallas_call(functools.partial(kernel, (ny, nz, nt, n_tb, n_sb, slots,...]
    dynamic_slice x64 -> x0, local copies, waits for them, and re-layouts: 49.2 us -> none  [the longest x32 25 us: step(): own_g = lax.dynamic_slice_in_dim(own_ids, start, group_slots)]
    reduce_max x64 -> x0, other arithmetic: 33.3 us -> none  [the longest x32 26.3 us: step(): jnp.max(jnp.where(own_hit[:, :, None], new_peak[None, :, :], lowest), axi...]
    all_gather x2 -> x0, blocking collectives: 29 us -> none  [the longest x1 20.1 us: local(): lax.all_gather(source_points, 'tgt', axis=1, tiled=True)]
    add x16 -> x0, other arithmetic: 28.8 us -> none  [step(): pick_rows(far_hit, far_sq)[:, :, None]]
  transfers between devices with their start and end apart: 2 -> 0, of which waited for: 2 -> 0; matrix products, arithmetic and copies ran while one was open for 0% -> 0% of each run, Pallas kernels for 0% -> 0%
where the time goes in v1:
time: 73.4 us; the launch traced here: 73.1 us
  Pallas kernels  64.1 us (87%)
  local copies, waits for them, and re-layouts  7.65 us (10%)
  between operations  1.3 us (2%)
    pallas_call x1, Pallas kernels, local(): pl.pallas_call(functools.partial(kernel, (ny, nz, nt, n_tb, n_sb, slots,...  64.1 us
    unnamed x16, local copies, waits for them, and re-layouts  7.65 us

profile of v1, /device:TPU:1, one launch (start us, length us, event | category | flops | bytes accessed | tf_op | source)
XLA Modules:
  0.0 73.1 jit_solution(17233546808089816090)
XLA Ops:
  1.3 0.0 copy-start
  1.3 2.0 %copy-done = f32[50,16384]{1,0:T(8,128)S(1)} copy-done((f32[50,16384]{1,0:T(8,128)S(1)}, f32[50,16384]{1,0:T(8,128)}, u32[]{:S(2)}) %copy-start) | copy-done | bytes 3276824
  3.3 0.0 copy-start.1
  3.3 0.8 %copy-done.1 = f32[16384]{0:T(1024)S(1)} copy-done((f32[16384]{0:T(1024)S(1)}, f32[16384]{0:T(1024)}, u32[]{:S(2)}) %copy-start.1) | copy-done | bytes 65560
  4.2 0.0 copy-start.2
  4.2 0.8 %copy-done.2 = f32[50,256]{1,0:T(8,128)S(1)} copy-done((f32[50,256]{1,0:T(8,128)S(1)}, f32[50,256]{1,0:T(8,128)}, u32[]{:S(2)}) %copy-start.2) | copy-done | bytes 51224
  5.0 0.0 copy-start.3
  5.0 0.7 copy-done.3
  5.7 0.0 copy-start.4
  5.7 0.7 copy-done.4
  6.4 0.0 copy-start.5
  6.4 0.7 copy-done.5
  7.0 0.0 copy-start.6
  7.0 0.7 copy-done.6
  7.7 64.1 %shard_map.95 = (f32[128,128]{1,0:T(8,128)S(1)}, f32[16,128]{1,0:T(8,128)S(1)}) custom-call(s32[256]{0:T(256)S(1)} %bitcast.15, s32[256]{0:T(256)S(1)} %bitcast.17, s32[1]{0:T(128)} %bitcast.10.count_ref, s32[1,256]{1,0:T(1,128)S(1)} %bitcast.16, s32[1,256]{1,0:T(1,128)S(1)} %bitcast.18, f32[50,256]{1,0:T(8,128)S(1)} %copy-done.2, f32[1,256]{1,0:T(1,128)S(1)} %bitcast.19, ...), custom_call_target="tpu_custom_call" | custom-call | tf_op jit(solution)/shard_map/pallas_call | solution.py:285
  71.8 0.6 copy.13
  72.5 0.6 copy.14
Async XLA Ops:
  1.3 2.0 %copy-start = (f32[50,16384]{1,0:T(8,128)S(1)}, f32[50,16384]{1,0:T(8,128)}, u32[]{:S(2)}) copy-start(f32[50,16384]{1,0:T(8,128)} %tpts_hbm.1) | copy-start | bytes 9830404
  3.3 0.8 %copy-start.1 = (f32[16384]{0:T(1024)S(1)}, f32[16384]{0:T(1024)}, u32[]{:S(2)}) copy-start(f32[16384]{0:T(1024)} %param.12) | copy-start | bytes 196612
  4.2 0.8 %copy-start.2 = (f32[50,256]{1,0:T(8,128)S(1)}, f32[50,256]{1,0:T(8,128)}, u32[]{:S(2)}) copy-start(f32[50,256]{1,0:T(8,128)} %spts.1) | copy-start | bytes 153604
  5.0 0.7 copy-start.3
  5.7 0.7 copy-start.4
  6.4 0.7 copy-start.5
  7.0 0.7 copy-start.6

commit v2 on v1

v2 whole, which is shorter than its diff:
```python
import functools
import math

import jax
import jax.numpy as jnp
from jax import lax
from jax.experimental import pallas as pl
from jax.experimental.pallas import tpu as pltpu
from jax.sharding import PartitionSpec as P

BLOCK = 128
HALF = 64
ROW_U = 50
ROW_F = 54
LOG2E = 1.4426950408889634
LN2 = 0.6931471805599453
SCALE = 2.0 * LOG2E
ROOT = math.sqrt(2.0 * SCALE)
LOWEST = -1.0e30
UNROLL = 32
CHUNKS = 4
MESH = pl.DeviceIdType.MESH
f32 = jnp.float32
bf16 = jnp.bfloat16


def split(x):
    high = x.astype(bf16)
    return high, (x - high.astype(f32)).astype(bf16)


def residue(x):
    high, low = split(x)
    return x - high.astype(f32) - low.astype(f32)


def merge(parts):
    top = jnp.max(parts, axis=0)
    return top + jnp.log2(jnp.sum(jnp.exp2(parts - top[None]), axis=0))


def column_lse(a, r):
    lhs = jnp.concatenate([a, a], axis=1)
    rhs = jnp.concatenate([r[:HALF], r[:HALF], r[HALF:], r[HALF:]], axis=0)
    score = jnp.dot(lhs, rhs, preferred_element_type=f32)
    top = jnp.max(score, axis=0, keepdims=True)
    return top + jnp.log2(jnp.sum(jnp.exp2(score - top), axis=0, keepdims=True))


def owner_pass(owners, first, slots, id_of, id_row, lse, peak, scaled):
    index = lax.broadcasted_iota(jnp.int32, (owners, BLOCK), 0)

    def lift(k, top):
        for step in range(8):
            p = first + k * 8 + step
            row = jnp.broadcast_to(lse[pl.ds(p, 1), :], (owners, BLOCK))
            top = jnp.maximum(top, jnp.where(index == id_of(p), row, LOWEST))
        return top

    top = lax.fori_loop(0, slots // 8, lift, jnp.full((owners, BLOCK), LOWEST, f32))
    peak[0:owners, :] = top

    def scale(k, carry):
        at = first + k * 16
        tops = jnp.concatenate([peak[pl.ds(id_of(at + step), 1), :] for step in range(16)], axis=0)
        rows = pl.ds(pl.multiple_of(at, 16), 16)
        scaled[rows, :] = jnp.exp2(lse[rows, :] - tops)
        return carry

    lax.fori_loop(0, slots // 16, scale, 0)
    hit = lax.broadcasted_iota(jnp.int32, (owners, slots), 0) == id_row
    pick = jnp.where(hit, 1.0, 0.0).astype(bf16)
    high, low = split(scaled[first : first + slots, :])
    total = jnp.dot(pick, high, preferred_element_type=f32) + jnp.dot(
        pick, low, preferred_element_type=f32
    )
    return top + jnp.log2(total)


def kernel(
    dims,
    spts_hbm, spot_hbm, slogw_hbm, tpts_hbm, tlogw_hbm, src_hbm, tgt_hbm, count_hbm,
    out_t, out_s,
    spts, spot, slogw, tlogw, ids_src, ids_tgt, count_ref, row_src, row_tgt, base_vec, base_src,
    tpts, xbuf, r_tgt, a_tgt, r_src, a_src, y_sq, lse, peak, scaled,
    extra, part, recv_y, comb, recv_z, full, rowpart, recv_x,
    load_sem, chunk_sem, base_sem, gather_send, gather_recv, relay_send,
    y_send, y_recv, z_send, z_recv, g_send, g_recv, x_send, x_recv,
):
    ny, nz, nt, n_tb, n_sb, slots, pc = dims
    nx = nt // 2
    me_s, me_t = lax.axis_index("src"), lax.axis_index("tgt")
    my_y, my_z = lax.rem(me_s, ny), lax.div(me_s, ny)
    my_x, my_c = lax.div(me_t, 2), lax.rem(me_t, 2)
    per_y = n_tb // ny
    shard_blocks = n_sb // nt
    n_extra = slots - n_tb

    def along_y(d):
        return (my_z * ny + lax.rem(my_y + d, ny), me_t)

    def along_z(d):
        return (lax.rem(my_z + d, nz) * ny + my_y, me_t)

    def along_t(d):
        return (me_s, lax.rem(me_t + d, nt))

    barrier = pltpu.get_barrier_semaphore()
    peers = (
        [along_t(d) for d in range(1, nt)]
        + [along_y(d) for d in range(1, ny)]
        + [along_z(d) for d in range(1, nz)]
    )
    for peer in peers:
        pl.semaphore_signal(barrier, inc=1, device_id=peer, device_id_type=MESH)

    pairs = [
        (spts_hbm, spts), (spot_hbm, spot), (src_hbm.at[0], row_src), (tgt_hbm.at[0], row_tgt),
        (src_hbm.at[0], ids_src), (tgt_hbm.at[0], ids_tgt), (count_hbm, count_ref),
        (slogw_hbm, slogw), (tlogw_hbm, tlogw),
    ]
    small = [pltpu.make_async_copy(a, b, load_sem.at[k]) for k, (a, b) in enumerate(pairs)]
    for load in small:
        load.start()
    width = n_tb * BLOCK // CHUNKS
    loads = []
    for c in range(CHUNKS):
        cols = pl.ds(c * width, width)
        load = pltpu.make_async_copy(tpts_hbm.at[:, cols], tpts.at[:, cols], chunk_sem.at[c])
        load.start()
        loads.append(load)
    small[0].wait()
    small[1].wait()

    x = spts[...] * ROOT
    pot = spot[...]
    cells = pot.shape[1]
    u = SCALE * pot - 0.5 * jnp.sum(x * x, axis=0, keepdims=True)
    one = jnp.ones((1, cells), f32)
    xbuf[me_t] = jnp.concatenate([x, u, residue(u), one, one, pot, 0.0 * one], axis=0)

    pl.semaphore_wait(barrier, len(peers))

    def remote(src, dst, send, recv, where):
        return pltpu.make_async_remote_copy(
            src_ref=src, dst_ref=dst, send_sem=send, recv_sem=recv,
            device_id=where, device_id_type=MESH,
        )

    def chip(d):
        return (me_s, lax.rem(my_x + d, nx) * 2 + my_c)

    other_core = (me_s, my_x * 2 + 1 - my_c)
    mine = xbuf.at[me_t]
    order = sorted(range(1, nx), key=lambda d: -min(d, nx - d))
    sent = [remote(mine, mine, gather_send.at[d], gather_recv.at[me_t], chip(d)) for d in order]
    sent.append(remote(mine, mine, gather_send.at[0], gather_recv.at[me_t], other_core))
    for copy in sent:
        copy.start()

    def arrived(slot, sem, where):
        remote(slot, slot, gather_send.at[0], sem, where).wait_recv()

    for load in small[2:]:
        load.wait()
    count = count_ref[0, 0]
    turned_t = jnp.broadcast_to(row_tgt[:, 0:n_tb], (n_tb, n_tb)).T
    turned_s = jnp.broadcast_to(row_src[:, 0:n_tb], (n_tb, n_tb)).T
    owner = lax.broadcasted_iota(jnp.int32, (n_tb, n_tb), 1)
    base_vec[...] = jnp.sum(jnp.where(turned_t == owner, turned_s, 0), axis=0, keepdims=True)
    base_copy = pltpu.make_async_copy(base_vec, base_src, base_sem)
    base_copy.start()

    tail = lax.broadcasted_iota(jnp.int32, (HALF - pc, BLOCK), 0)
    tail = jnp.where(tail < 2, 1.0, 0.0)

    def prepare(k, carry):
        for step in range(4):
            b = k * 4 + step
            y = tpts[:, pl.ds(pl.multiple_of(b * BLOCK, BLOCK), BLOCK)] * ROOT
            y_sq[pl.ds(b, 1), :] = 0.5 * jnp.sum(y * y, axis=0, keepdims=True)
            high, low = split(jnp.concatenate([y, tail], axis=0))
            r_tgt[b] = jnp.concatenate([high, low], axis=0)
        return carry

    per_chunk = n_tb // CHUNKS // 4
    for c in range(CHUNKS):
        loads[c].wait()
        lax.fori_loop(c * per_chunk, (c + 1) * per_chunk, prepare, 0)

    zeros = jnp.zeros((HALF - 56, BLOCK), f32)

    def source(t):
        for h in range(shard_blocks):
            b = t * shard_blocks + h
            xs = xbuf[t, :, h * BLOCK : (h + 1) * BLOCK]
            high, low = split(jnp.concatenate([xs, zeros], axis=0))
            both = jnp.concatenate([high, low], axis=0)
            r_src[b] = both
            a_src[b] = both.T

    source(me_t)
    relays = []
    for d in reversed(order):
        t = lax.rem(my_x + d, nx) * 2 + my_c
        arrived(xbuf.at[t], gather_recv.at[t], chip(d))
        relay = remote(xbuf.at[t], xbuf.at[t], relay_send.at[d], gather_recv.at[t], other_core)
        relay.start()
        relays.append(relay)
        source(t)
    for d in [0] + order[::-1]:
        t = lax.rem(my_x + d, nx) * 2 + 1 - my_c
        arrived(xbuf.at[t], gather_recv.at[t], other_core)
        source(t)
    base_copy.wait()

    def far_columns(k, carry):
        for step in range(UNROLL):
            p = n_tb + k * UNROLL + step
            row = column_lse(a_src[ids_src[0, p]], r_tgt[ids_tgt[0, p]])
            lse[pl.ds(p, 1), :] = jnp.where(p < count, row, LOWEST)
        return carry

    lax.fori_loop(0, n_extra // UNROLL, far_columns, 0)
    extra[...] = owner_pass(
        n_tb, n_tb, n_extra, lambda p: ids_tgt[0, p], row_tgt[:, n_tb:], lse, peak, scaled
    )

    def band(y):
        return pl.ds(pl.multiple_of(y * per_y, per_y), per_y)

    def to_y(d):
        y = lax.rem(my_y + d, ny)
        return remote(part.at[band(y)], recv_y.at[my_y], y_send.at[d], y_recv.at[my_y], along_y(d))

    def near_columns(m, carry):
        ds = (ny // 2 - m, lax.rem(ny // 2 + 1 + m, ny))
        for d in ds:
            start = lax.rem(my_y + d, ny) * per_y
            for step in range(per_y):
                b = start + step
                lse[pl.ds(b, 1), :] = column_lse(a_src[base_src[0, b]], r_tgt[b])
        for d in ds:
            rows = band(lax.rem(my_y + d, ny))
            part[rows, :] = merge(jnp.stack([lse[rows, :], extra[rows, :]]))
        to_y(ds[0]).start()

        @pl.when(m < ny // 2 - 1)
        def _():
            to_y(ds[1]).start()

        return carry

    lax.fori_loop(0, ny // 2, near_columns, 0)
    recv_y[my_y] = part[band(my_y), :]

    def collect(n, me, where, dst, send, recv):
        for d in range(1, n):
            other = lax.rem(me + d, n)
            remote(dst(other), dst(other), send.at[d], recv.at[other], where(d)).wait_recv()

    collect(ny, my_y, along_y, lambda y: recv_y.at[y], y_send, y_recv)
    comb[...] = merge(recv_y[...])

    def to_z(d):
        return remote(comb, recv_z.at[my_z], z_send.at[d], z_recv.at[my_z], along_z(d))

    def by_distance(n):
        return sorted(range(1, n), key=lambda d: -min(d, n - d))

    for d in by_distance(nz):
        to_z(d).start()
    recv_z[my_z] = comb[...]
    collect(nz, my_z, along_z, lambda z: recv_z.at[z], z_send, z_recv)
    full[band(my_y), :] = merge(recv_z[...])

    def to_all(d):
        rows = full.at[band(my_y)]
        return remote(rows, rows, g_send.at[d], g_recv.at[my_y], along_y(d))

    for d in by_distance(ny):
        to_all(d).start()

    line = lax.broadcasted_iota(jnp.int32, (16, BLOCK), 0)

    def near_rows(k, carry):
        d = lax.rem(lax.div(k + 1, 2) * (1 - 2 * lax.rem(k + 1, 2)) * -1 + 2 * ny, ny)
        y = lax.rem(my_y + d, ny)
        rows = band(y)

        @pl.when(k > 0)
        def _():
            slot = full.at[rows]
            remote(slot, slot, g_send.at[d], g_recv.at[y], along_y(d)).wait_recv()

        total = full[rows, :]
        weight = tlogw[rows, :]
        out_t[rows, :] = 0.5 * weight - (0.5 * LN2) * (total - y_sq[rows, :])
        v = LOG2E * weight - total
        v_high, v_low = split(v)
        rest = residue(v)
        v_high, v_low = v_high.astype(f32), v_low.astype(f32)
        for step in range(per_y):
            b = y * per_y + step
            r = r_tgt[b]
            one = slice(step, step + 1)
            high = jnp.where(line == 5, rest[one], r[48:64].astype(f32))
            high = jnp.where(line == 4, v_high[one], high)
            low = jnp.where(line == 4, v_low[one], r[112:128].astype(f32))
            both = jnp.concatenate([r[:48], high.astype(bf16), r[64:112], low.astype(bf16)], axis=0)
            turned = both.T
            a_tgt[b] = turned
            lse[pl.ds(b, 1), :] = column_lse(turned, r_src[base_src[0, b]])
        return carry

    lax.fori_loop(0, ny, near_rows, 0)

    def far_rows(k, carry):
        for step in range(UNROLL):
            p = n_tb + k * UNROLL + step
            row = column_lse(a_tgt[ids_tgt[0, p]], r_src[ids_src[0, p]])
            lse[pl.ds(p, 1), :] = jnp.where(p < count, row, LOWEST)
        return carry

    lax.fori_loop(0, n_extra // UNROLL, far_rows, 0)
    near = owner_pass(n_sb, 0, n_tb, lambda p: base_src[0, p], base_vec[...], lse, peak, scaled)
    far = owner_pass(
        n_sb, n_tb, n_extra, lambda p: ids_src[0, p], row_src[:, n_tb:], lse, peak, scaled
    )
    rowpart[...] = merge(jnp.stack([near, far]))

    def to_t(d):
        return remote(rowpart, recv_x.at[me_t], x_send.at[d], x_recv.at[me_t], along_t(d))

    for d in by_distance(nt):
        to_t(d).start()
    recv_x[me_t] = rowpart[...]
    potential = jnp.concatenate(
        [
            xbuf[t, ROW_F : ROW_F + 1, h * BLOCK : (h + 1) * BLOCK]
            for t in range(nt)
            for h in range(shard_blocks)
        ],
        axis=0,
    )
    collect(nt, me_t, along_t, lambda t: recv_x.at[t], x_send, x_recv)
    out_s[...] = potential + 0.5 * slogw[...] - (0.5 * LN2) * merge(recv_x[...])

    for copy in sent + relays:
        copy.wait_send()
    for n, to in ((ny, to_y), (nz, to_z), (ny, to_all), (nt, to_t)):
        for d in range(1, n):
            to(d).wait_send()


def local(
    n_src,
    n_tgt,
    source_points,
    source_potential,
    source_logw,
    target_points,
    target_logw,
    pair_source,
    pair_target,
    pair_count,
):
    pc, cells = source_points.shape
    n_tb = target_points.shape[1] // BLOCK
    n_sb = source_logw.shape[0] // BLOCK
    slots = pair_source.shape[-1]
    ny = math.isqrt(n_src)
    nz = n_src // ny
    nt = n_tgt
    per_y = n_tb // ny
    vmem = pl.BlockSpec(memory_space=pltpu.VMEM)
    dma = pltpu.SemaphoreType.DMA
    out_t, out_s = pl.pallas_call(
        functools.partial(kernel, (ny, nz, nt, n_tb, n_sb, slots, pc)),
        out_shape=(
            jax.ShapeDtypeStruct((n_tb, BLOCK), f32),
            jax.ShapeDtypeStruct((n_sb, BLOCK), f32),
        ),
        in_specs=[pl.BlockSpec(memory_space=pltpu.HBM)] * 8,
        out_specs=(vmem, vmem),
        scratch_shapes=[
            pltpu.VMEM((pc, cells), f32),
            pltpu.VMEM((1, cells), f32),
            pltpu.VMEM((n_sb, BLOCK), f32),
            pltpu.VMEM((n_tb, BLOCK), f32),
            pltpu.SMEM((1, slots), jnp.int32),
            pltpu.SMEM((1, slots), jnp.int32),
            pltpu.SMEM((1, 1), jnp.int32),
            pltpu.VMEM((1, slots), jnp.int32),
            pltpu.VMEM((1, slots), jnp.int32),
            pltpu.VMEM((1, n_tb), jnp.int32),
            pltpu.SMEM((1, n_tb), jnp.int32),
            pltpu.VMEM((pc, n_tb * BLOCK), f32),
            pltpu.VMEM((nt, 56, cells), f32),
            pltpu.VMEM((n_tb, BLOCK, BLOCK), bf16),
            pltpu.VMEM((n_tb, BLOCK, BLOCK), bf16),
            pltpu.VMEM((n_sb, BLOCK, BLOCK), bf16),
            pltpu.VMEM((n_sb, BLOCK, BLOCK), bf16),
            pltpu.VMEM((n_tb, BLOCK), f32),
            pltpu.VMEM((slots, BLOCK), f32),
            pltpu.VMEM((n_tb, BLOCK), f32),
            pltpu.VMEM((slots, BLOCK), f32),
            pltpu.VMEM((n_tb, BLOCK), f32),
            pltpu.VMEM((n_tb, BLOCK), f32),
            pltpu.VMEM((ny, per_y, BLOCK), f32),
            pltpu.VMEM((per_y, BLOCK), f32),
            pltpu.VMEM((nz, per_y, BLOCK), f32),
            pltpu.VMEM((n_tb, BLOCK), f32),
            pltpu.VMEM((n_sb, BLOCK), f32),
            pltpu.VMEM((nt, n_sb, BLOCK), f32),
            dma((9,)),
            dma((CHUNKS,)),
            dma,
            dma((nt,)), dma((nt,)), dma((nt,)),
            dma((ny,)), dma((ny,)),
            dma((nz,)), dma((nz,)),
            dma((ny,)), dma((ny,)),
            dma((nt,)), dma((nt,)),
        ],
        compiler_params=pltpu.CompilerParams(
            collective_id=0, has_side_effects=True, vmem_limit_bytes=60 * 2**20
        ),
    )(
        source_points,
        source_potential.reshape(1, cells),
        source_logw.reshape(n_sb, BLOCK),
        target_points,
        target_logw.reshape(n_tb, BLOCK),
        pair_source,
        pair_target,
        pair_count,
    )
    return out_t.reshape(-1), out_s.reshape(-1)


def solution(mesh):
    placed = (
        P(None, ("src", "tgt")),
        P(("src", "tgt")),
        P("src"),
        P(None, "tgt"),
        P("tgt"),
        P("src", "tgt", None),
        P("src", "tgt", None),
        P("src", "tgt"),
    )
    return jax.shard_map(
        functools.partial(local, mesh.shape["src"], mesh.shape["tgt"]),
        mesh=mesh,
        in_specs=placed,
        out_specs=(P("tgt"), P("src")),
        check_vma=False,
    )
```

time: 73.4 us -> 55.7 us (0.76)
  Pallas kernels: 64.1 us -> 51.4 us
  local copies, waits for them, and re-layouts: 7.65 us -> 2.77 us
    pallas_call x1, Pallas kernels: 64.1 us -> 51.4 us  [local(): pl.pallas_call(functools.partial(kernel, (ny, nz, nt, n_tb, n_sb, slots,...]
    unnamed x16 -> x2, local copies, waits for them, and re-layouts: 7.65 us -> 2.77 us
where the time goes in v2:
time: 55.7 us; the launch traced here: 55.5 us
  Pallas kernels  51.4 us (92%)
  local copies, waits for them, and re-layouts  2.77 us (5%)
  between operations  1.29 us (2%)
    pallas_call x1, Pallas kernels, local(): pl.pallas_call(functools.partial(kernel, (ny, nz, nt, n_tb, n_sb, slots,...  51.4 us
    unnamed x2, local copies, waits for them, and re-layouts  2.77 us

profile of v2, /device:TPU:1, one launch (start us, length us, event | category | flops | bytes accessed | tf_op | source)
XLA Modules:
  0.0 55.5 jit_solution(8973349875127865319)
XLA Ops:
  1.3 51.4 %shard_map.95 = (f32[128,128]{1,0:T(8,128)}, f32[16,128]{1,0:T(8,128)}) custom-call(f32[50,256]{1,0:T(8,128)} %spts_hbm.1, f32[1,256]{1,0:T(1,128)} %bitcast.9, f32[16,128]{1,0:T(8,128)} %bitcast.7, f32[50,16384]{1,0:T(8,128)} %tpts_hbm.1, f32[128,128]{1,0:T(8,128)} %bitcast.5, s32[1,1,256]{2,1,0:T(1,128)} %src_hbm.1, s32[1,1,256]{2,1,0:T(1,128)} %tgt_hbm.1, ...), custom_call_target="tpu_custom_call" | custom-call | tf_op jit(solution)/shard_map/pallas_call | solution.py:378
  52.7 1.5 %copy.13 = f32[16384]{0:T(1024)} copy(f32[16384]{0:T(1024)} %bitcast.6) | data formatting | bytes 131072
  54.2 1.3 %copy.14 = f32[2048]{0:T(1024)} copy(f32[2048]{0:T(1024)} %bitcast.8) | data formatting | bytes 16384

commit v3 on v2

--- a/solution.py
+++ b/solution.py
@@ -17,7 +17,9 @@
 SCALE = 2.0 * LOG2E
 ROOT = math.sqrt(2.0 * SCALE)
 LOWEST = -1.0e30
-UNROLL = 32
+STEP = 64.0
+MIDDLE = 6.0
+UNROLL = 128
 CHUNKS = 4
 MESH = pl.DeviceIdType.MESH
 f32 = jnp.float32
@@ -47,42 +49,50 @@
     return top + jnp.log2(jnp.sum(jnp.exp2(score - top), axis=0, keepdims=True))
 
 
-def owner_pass(owners, first, slots, id_of, id_row, lse, peak, scaled):
-    index = lax.broadcasted_iota(jnp.int32, (owners, BLOCK), 0)
-
-    def lift(k, top):
-        for step in range(8):
-            p = first + k * 8 + step
-            row = jnp.broadcast_to(lse[pl.ds(p, 1), :], (owners, BLOCK))
-            top = jnp.maximum(top, jnp.where(index == id_of(p), row, LOWEST))
-        return top
-
-    top = lax.fori_loop(0, slots // 8, lift, jnp.full((owners, BLOCK), LOWEST, f32))
-    peak[0:owners, :] = top
-
-    def scale(k, carry):
-        at = first + k * 16
-        tops = jnp.concatenate([peak[pl.ds(id_of(at + step), 1), :] for step in range(16)], axis=0)
-        rows = pl.ds(pl.multiple_of(at, 16), 16)
-        scaled[rows, :] = jnp.exp2(lse[rows, :] - tops)
-        return carry
-
-    lax.fori_loop(0, slots // 16, scale, 0)
-    hit = lax.broadcasted_iota(jnp.int32, (owners, slots), 0) == id_row
-    pick = jnp.where(hit, 1.0, 0.0).astype(bf16)
-    high, low = split(scaled[first : first + slots, :])
-    total = jnp.dot(pick, high, preferred_element_type=f32) + jnp.dot(
-        pick, low, preferred_element_type=f32
+def raise_peaks(top, rows, ids):
+    index = lax.broadcasted_iota(jnp.int32, top.shape, 0)
+    tops = [top]
+    for row, owner in zip(rows, ids):
+        tops.append(jnp.where(index == owner, jnp.broadcast_to(row, top.shape), LOWEST))
+    while len(tops) > 1:
+        tops = [functools.reduce(jnp.maximum, tops[i : i + 2]) for i in range(0, len(tops), 2)]
+    return tops[0]
+
+
+def owner_sums(top, lse, pick, gather):
+    high, low = split(top)
+    parts = [high, low, residue(top).astype(bf16)]
+    spare = gather.shape[1] - 3 * top.shape[0]
+    if spare > 0:
+        parts.append(jnp.zeros((spare, BLOCK), bf16))
+    tops = jnp.dot(gather[...], jnp.concatenate(parts, axis=0), preferred_element_type=f32)
+    high, low = split(jnp.exp2(lse - tops))
+    total = jnp.dot(pick[...], high, preferred_element_type=f32) + jnp.dot(
+        pick[...], low, preferred_element_type=f32
     )
     return top + jnp.log2(total)
+
+
+def owner_steps(lse, pick, gather):
+    step = jnp.clip(jnp.floor(lse * (1.0 / STEP)) - MIDDLE, -30.0, 30.0)
+    power = jnp.where(lse > 0.5 * LOWEST, jnp.exp2(4.0 * step), 0.0)
+    total = jnp.dot(pick[...], power.astype(bf16), preferred_element_type=f32)
+    largest = jnp.floor(0.25 * (jnp.log2(jnp.maximum(total, 2.0**-122)) + 0.04))
+    edge = STEP * (largest + MIDDLE + 1.0)
+    edges = jnp.dot(gather[...], edge.astype(bf16), preferred_element_type=f32)
+    high, low = split(jnp.exp2(lse - edges))
+    total = jnp.dot(pick[...], high, preferred_element_type=f32) + jnp.dot(
+        pick[...], low, preferred_element_type=f32
+    )
+    return edge + jnp.log2(total)
 
 
 def kernel(
     dims,
     spts_hbm, spot_hbm, slogw_hbm, tpts_hbm, tlogw_hbm, src_hbm, tgt_hbm, count_hbm,
     out_t, out_s,
-    spts, spot, slogw, tlogw, ids_src, ids_tgt, count_ref, row_src, row_tgt, base_vec, base_src,
-    tpts, xbuf, r_tgt, a_tgt, r_src, a_src, y_sq, lse, peak, scaled,
+    spts, spot, slogw, tlogw, ids_src, ids_tgt, count_ref, row_src, row_tgt, base_vec, row_ids,
+    tpts, xbuf, r_tgt, a_tgt, r_src, a_src, y_sq, lse, far, pick_t, gather_t, pick_s, gather_s,
     extra, part, recv_y, comb, recv_z, full, rowpart, recv_x,
     load_sem, chunk_sem, base_sem, gather_send, gather_recv, relay_send,
     y_send, y_recv, z_send, z_recv, g_send, g_recv, x_send, x_recv,
@@ -167,9 +177,25 @@
     turned_t = jnp.broadcast_to(row_tgt[:, 0:n_tb], (n_tb, n_tb)).T
     turned_s = jnp.broadcast_to(row_src[:, 0:n_tb], (n_tb, n_tb)).T
     owner = lax.broadcasted_iota(jnp.int32, (n_tb, n_tb), 1)
-    base_vec[...] = jnp.sum(jnp.where(turned_t == owner, turned_s, 0), axis=0, keepdims=True)
-    base_copy = pltpu.make_async_copy(base_vec, base_src, base_sem)
+    base_row = jnp.sum(jnp.where(turned_t == owner, turned_s, 0), axis=0, keepdims=True)
+    base_vec[:, 0:n_tb] = base_row
+    base_vec[:, n_tb:] = row_src[:, n_tb:]
+    base_copy = pltpu.make_async_copy(base_vec, row_ids, base_sem)
     base_copy.start()
+
+    def one_hot(flags):
+        return jnp.where(flags, 1.0, 0.0).astype(bf16)
+
+    further_t, further_s = row_tgt[:, n_tb:], row_src[:, n_tb:]
+    pick_t[...] = one_hot(lax.broadcasted_iota(jnp.int32, (n_tb, n_extra), 0) == further_t)
+    column = jnp.broadcast_to(further_t, (n_tb, n_extra)).T
+    gather_t[...] = one_hot(lax.broadcasted_iota(jnp.int32, (n_extra, n_tb), 1) == column)
+    lane = lax.broadcasted_iota(jnp.int32, (BLOCK, BLOCK), 1)
+    lane = jnp.where(lane < 3 * n_sb, lax.rem(lane, n_sb), -1)
+    for at, ids in ((0, base_row), (n_tb, further_s)):
+        n = ids.shape[1]
+        pick_s[:, at : at + n] = one_hot(lax.broadcasted_iota(jnp.int32, (n_sb, n), 0) == ids)
+        gather_s[at : at + n, :] = one_hot(jnp.broadcast_to(ids, (BLOCK, n)).T == lane[0:n])
 
     tail = lax.broadcasted_iota(jnp.int32, (HALF - pc, BLOCK), 0)
     tail = jnp.where(tail < 2, 1.0, 0.0)
@@ -216,15 +242,12 @@
 
     def far_columns(k, carry):
         for step in range(UNROLL):
-            p = n_tb + k * UNROLL + step
-            row = column_lse(a_src[ids_src[0, p]], r_tgt[ids_tgt[0, p]])
-            lse[pl.ds(p, 1), :] = jnp.where(p < count, row, LOWEST)
+            p = k * UNROLL + step
+            row = column_lse(a_src[ids_src[0, n_tb + p]], r_tgt[ids_tgt[0, n_tb + p]])
+            far[pl.ds(p, 1), :] = jnp.where(n_tb + p < count, row, LOWEST)
         return carry
 
     lax.fori_loop(0, n_extra // UNROLL, far_columns, 0)
-    extra[...] = owner_pass(
-        n_tb, n_tb, n_extra, lambda p: ids_tgt[0, p], row_tgt[:, n_tb:], lse, peak, scaled
-    )
 
     def band(y):
         return pl.ds(pl.multiple_of(y * per_y, per_y), per_y)
@@ -233,25 +256,28 @@
         y = lax.rem(my_y + d, ny)
         return remote(part.at[band(y)], recv_y.at[my_y], y_send.at[d], y_recv.at[my_y], along_y(d))
 
-    def near_columns(m, carry):
-        ds = (ny // 2 - m, lax.rem(ny // 2 + 1 + m, ny))
+    def near_columns(ds):
+        bands = [lax.rem(my_y + d, ny) for d in ds]
+        for y in bands:
+            for step in range(per_y):
+                b = y * per_y + step
+                lse[pl.ds(b, 1), :] = column_lse(a_src[row_ids[0, b]], r_tgt[b])
+        for y in bands:
+            part[band(y), :] = merge(jnp.stack([lse[band(y), :], extra[band(y), :]]))
         for d in ds:
-            start = lax.rem(my_y + d, ny) * per_y
-            for step in range(per_y):
-                b = start + step
-                lse[pl.ds(b, 1), :] = column_lse(a_src[base_src[0, b]], r_tgt[b])
-        for d in ds:
-            rows = band(lax.rem(my_y + d, ny))
-            part[rows, :] = merge(jnp.stack([lse[rows, :], extra[rows, :]]))
-        to_y(ds[0]).start()
-
-        @pl.when(m < ny // 2 - 1)
-        def _():
-            to_y(ds[1]).start()
-
+            if not (isinstance(d, int) and d == 0):
+                to_y(d).start()
+
+    def near_pair(m, carry):
+        near_columns([ny // 2 - m, ny // 2 + 1 + m])
         return carry
 
-    lax.fori_loop(0, ny // 2, near_columns, 0)
+    extra[...] = owner_steps(far[...], pick_t, gather_t)
+    if ny > 2:
+        near_columns([ny // 2, ny // 2 + 1])
+        lax.fori_loop(1, ny // 2 - 1, near_pair, 0)
+    near_columns([1])
+    near_columns([0])
     recv_y[my_y] = part[band(my_y), :]
 
     def collect(n, me, where, dst, send, recv):
@@ -283,51 +309,61 @@
 
     line = lax.broadcasted_iota(jnp.int32, (16, BLOCK), 0)
 
-    def near_rows(k, carry):
-        d = lax.rem(lax.div(k + 1, 2) * (1 - 2 * lax.rem(k + 1, 2)) * -1 + 2 * ny, ny)
-        y = lax.rem(my_y + d, ny)
-        rows = band(y)
-
-        @pl.when(k > 0)
-        def _():
-            slot = full.at[rows]
-            remote(slot, slot, g_send.at[d], g_recv.at[y], along_y(d)).wait_recv()
-
-        total = full[rows, :]
-        weight = tlogw[rows, :]
-        out_t[rows, :] = 0.5 * weight - (0.5 * LN2) * (total - y_sq[rows, :])
-        v = LOG2E * weight - total
-        v_high, v_low = split(v)
-        rest = residue(v)
-        v_high, v_low = v_high.astype(f32), v_low.astype(f32)
-        for step in range(per_y):
-            b = y * per_y + step
-            r = r_tgt[b]
-            one = slice(step, step + 1)
-            high = jnp.where(line == 5, rest[one], r[48:64].astype(f32))
-            high = jnp.where(line == 4, v_high[one], high)
-            low = jnp.where(line == 4, v_low[one], r[112:128].astype(f32))
-            both = jnp.concatenate([r[:48], high.astype(bf16), r[64:112], low.astype(bf16)], axis=0)
-            turned = both.T
-            a_tgt[b] = turned
-            lse[pl.ds(b, 1), :] = column_lse(turned, r_src[base_src[0, b]])
+    def near_rows(ds):
+        bands = [lax.rem(my_y + d, ny) for d in ds]
+        values = []
+        for y, d in zip(bands, ds):
+            rows = band(y)
+            if not (isinstance(d, int) and d == 0):
+                slot = full.at[rows]
+                remote(slot, slot, g_send.at[d], g_recv.at[y], along_y(d)).wait_recv()
+        for y in bands:
+            rows = band(y)
+            total = full[rows, :]
+            weight = tlogw[rows, :]
+            out_t[rows, :] = 0.5 * weight - (0.5 * LN2) * (total - y_sq[rows, :])
+            v = LOG2E * weight - total
+            high, low = split(v)
+            values.append((high.astype(f32), low.astype(f32), residue(v)))
+        for y, (v_high, v_low, rest) in zip(bands, values):
+            for step in range(per_y):
+                b = y * per_y + step
+                r = r_tgt[b]
+                one = slice(step, step + 1)
+                high = jnp.where(line == 5, rest[one], r[48:64].astype(f32))
+                high = jnp.where(line == 4, v_high[one], high)
+                low = jnp.where(line == 4, v_low[one], r[112:128].astype(f32))
+                both = [r[:48], high.astype(bf16), r[64:112], low.astype(bf16)]
+                turned = jnp.concatenate(both, axis=0).T
+                a_tgt[b] = turned
+                lse[pl.ds(b, 1), :] = column_lse(turned, r_src[row_ids[0, b]])
+
+    def near_row_pair(m, carry):
+        near_rows([m, ny - m])
         return carry
 
-    lax.fori_loop(0, ny, near_rows, 0)
+    near_rows([0])
+    lax.fori_loop(1, ny // 2, near_row_pair, 0)
+    near_rows([ny // 2])
 
     def far_rows(k, carry):
         for step in range(UNROLL):
-            p = n_tb + k * UNROLL + step
-            row = column_lse(a_tgt[ids_tgt[0, p]], r_src[ids_src[0, p]])
-            lse[pl.ds(p, 1), :] = jnp.where(p < count, row, LOWEST)
+            p = k * UNROLL + step
+            row = column_lse(a_tgt[ids_tgt[0, n_tb + p]], r_src[ids_src[0, n_tb + p]])
+            far[pl.ds(p, 1), :] = jnp.where(n_tb + p < count, row, LOWEST)
         return carry
 
     lax.fori_loop(0, n_extra // UNROLL, far_rows, 0)
-    near = owner_pass(n_sb, 0, n_tb, lambda p: base_src[0, p], base_vec[...], lse, peak, scaled)
-    far = owner_pass(
-        n_sb, n_tb, n_extra, lambda p: ids_src[0, p], row_src[:, n_tb:], lse, peak, scaled
-    )
-    rowpart[...] = merge(jnp.stack([near, far]))
+    def lift(part, first, k, top):
+        at = [k * 8 + step for step in range(8)]
+        ids = [row_ids[0, first + p] for p in at]
+        return raise_peaks(top, [part[pl.ds(p, 1), :] for p in at], ids)
+
+    row_peak = jnp.full((n_sb, BLOCK), LOWEST, f32)
+    row_peak = lax.fori_loop(0, n_tb // 8, functools.partial(lift, lse, 0), row_peak)
+    row_peak = lax.fori_loop(0, n_extra // 8, functools.partial(lift, far, n_tb), row_peak)
+    both = jnp.concatenate([lse[...], far[...]], axis=0)
+    rowpart[...] = owner_sums(row_peak, both, pick_s, gather_s)
 
     def to_t(d):
         return remote(rowpart, recv_x.at[me_t], x_send.at[d], x_recv.at[me_t], along_t(d))
@@ -373,13 +409,14 @@
     nz = n_src // ny
     nt = n_tgt
     per_y = n_tb // ny
+    n_extra = slots - n_tb
     vmem = pl.BlockSpec(memory_space=pltpu.VMEM)
     dma = pltpu.SemaphoreType.DMA
     out_t, out_s = pl.pallas_call(
         functools.partial(kernel, (ny, nz, nt, n_tb, n_sb, slots, pc)),
         out_shape=(
-            jax.ShapeDtypeStruct((n_tb, BLOCK), f32),
-            jax.ShapeDtypeStruct((n_sb, BLOCK), f32),
+            pltpu.VMEM((n_tb, BLOCK), f32),
+            pltpu.VMEM((n_sb, BLOCK), f32),
         ),
         in_specs=[pl.BlockSpec(memory_space=pltpu.HBM)] * 8,
         out_specs=(vmem, vmem),
@@ -393,8 +430,8 @@
             pltpu.SMEM((1, 1), jnp.int32),
             pltpu.VMEM((1, slots), jnp.int32),
             pltpu.VMEM((1, slots), jnp.int32),
-            pltpu.VMEM((1, n_tb), jnp.int32),
-            pltpu.SMEM((1, n_tb), jnp.int32),
+            pltpu.VMEM((1, slots), jnp.int32),
+            pltpu.SMEM((1, slots), jnp.int32),
             pltpu.VMEM((pc, n_tb * BLOCK), f32),
             pltpu.VMEM((nt, 56, cells), f32),
             pltpu.VMEM((n_tb, BLOCK, BLOCK), bf16),
@@ -402,9 +439,12 @@
             pltpu.VMEM((n_sb, BLOCK, BLOCK), bf16),
             pltpu.VMEM((n_sb, BLOCK, BLOCK), bf16),
             pltpu.VMEM((n_tb, BLOCK), f32),
-            pltpu.VMEM((slots, BLOCK), f32),
-            pltpu.VMEM((n_tb, BLOCK), f32),
-            pltpu.VMEM((slots, BLOCK), f32),
+            pltpu.VMEM((n_tb, BLOCK), f32),
+            pltpu.VMEM((n_extra, BLOCK), f32),
+            pltpu.VMEM((n_tb, n_extra), bf16),
+            pltpu.VMEM((n_extra, n_tb), bf16),
+            pltpu.VMEM((n_sb, slots), bf16),
+            pltpu.VMEM((slots, BLOCK), bf16),
             pltpu.VMEM((n_tb, BLOCK), f32),
             pltpu.VMEM((n_tb, BLOCK), f32),
             pltpu.VMEM((ny, per_y, BLOCK), f32),
@@ -423,16 +463,21 @@
             dma((nt,)), dma((nt,)),
         ],
         compiler_params=pltpu.CompilerParams(
-            collective_id=0, has_side_effects=True, vmem_limit_bytes=60 * 2**20
+            collective_id=0, has_side_effects=True, vmem_limit_bytes=40 * 2**20
         ),
     )(
-        source_points,
-        source_potential.reshape(1, cells),
-        source_logw.reshape(n_sb, BLOCK),
-        target_points,
-        target_logw.reshape(n_tb, BLOCK),
-        pair_source,
-        pair_target,
+        *(
+            pltpu.with_memory_space_constraint(operand, pltpu.HBM)
+            for operand in (
+                source_points,
+                source_potential.reshape(1, cells),
+                source_logw.reshape(n_sb, BLOCK),
+                target_points,
+                target_logw.reshape(n_tb, BLOCK),
+                pair_source,
+                pair_target,
+            )
+        ),
         pair_count,
     )
     return out_t.reshape(-1), out_s.reshape(-1)

time: 55.7 us -> 50.1 us (0.90)
  Pallas kernels: 51.4 us -> 47.5 us
  local copies, waits for them, and re-layouts: 2.77 us -> 1.23 us
    pallas_call x1, Pallas kernels: 51.4 us -> 47.5 us  [local(): pl.pallas_call(functools.partial(kernel, (ny, nz, nt, n_tb, n_sb, slots,...]
    unnamed x2, local copies, waits for them, and re-layouts: 2.77 us -> 1.23 us
where the time goes in v3:
time: 50.1 us; the launch traced here: 50 us
  Pallas kernels  47.5 us (95%)
  between operations  1.29 us (3%)
  local copies, waits for them, and re-layouts  1.23 us (2%)
    pallas_call x1, Pallas kernels, local(): pl.pallas_call(functools.partial(kernel, (ny, nz, nt, n_tb, n_sb, slots,...  47.5 us
    unnamed x2, local copies, waits for them, and re-layouts  1.23 us

profile of v3, /device:TPU:1, one launch (start us, length us, event | category | flops | bytes accessed | tf_op | source)
XLA Modules:
  0.0 50.0 jit_solution(12619084815977944359)
XLA Ops:
  1.3 47.5 %shard_map.95 = (f32[128,128]{1,0:T(8,128)S(1)}, f32[16,128]{1,0:T(8,128)S(1)}) custom-call(f32[50,256]{1,0:T(8,128)} %spts_hbm.1, f32[1,256]{1,0:T(1,128)} %bitcast.9, f32[16,128]{1,0:T(8,128)} %bitcast.8, f32[50,16384]{1,0:T(8,128)} %tpts_hbm.1, f32[128,128]{1,0:T(8,128)} %bitcast.7, s32[1,1,256]{2,1,0:T(1,128)} %src_hbm.1, s32[1,1,256]{2,1,0:T(1,128)} %tgt_hbm.1, ...), custom_call_target="tpu_custom_call" | custom-call | tf_op jit(solution)/shard_map/pallas_call | solution.py:415
  48.8 0.6 %copy.12 = f32[16384]{0:T(1024)} copy(f32[16384]{0:T(1024)S(1)} %bitcast.5) | data formatting | bytes 131072
  49.4 0.6 %copy.13 = f32[2048]{0:T(1024)} copy(f32[2048]{0:T(1024)S(1)} %bitcast.6) | data formatting | bytes 16384

commit v4 on v3

--- a/solution.py
+++ b/solution.py
@@ -39,6 +39,10 @@
 def merge(parts):
     top = jnp.max(parts, axis=0)
     return top + jnp.log2(jnp.sum(jnp.exp2(parts - top[None]), axis=0))
+
+
+def repeat(times, body, carry):
+    return body(0, carry) if times == 1 else lax.fori_loop(0, times, body, carry)
 
 
 def column_lse(a, r):
@@ -116,21 +120,34 @@
         return (me_s, lax.rem(me_t + d, nt))
 
     barrier = pltpu.get_barrier_semaphore()
+    def chip(d):
+        return (me_s, lax.rem(my_x + d, nx) * 2 + my_c)
+
+    other_core = (me_s, my_x * 2 + 1 - my_c)
+    order = sorted(range(1, nx), key=lambda d: -min(d, nx - d))
     peers = (
-        [along_t(d) for d in range(1, nt)]
+        [chip(d) for d in order]
+        + [other_core]
+        + [(me_s, lax.rem(my_x + d, nx) * 2 + 1 - my_c) for d in order]
         + [along_y(d) for d in range(1, ny)]
         + [along_z(d) for d in range(1, nz)]
     )
-    for peer in peers:
+    def greet(peer):
         pl.semaphore_signal(barrier, inc=1, device_id=peer, device_id_type=MESH)
 
+    for peer in peers[0:nx]:
+        greet(peer)
     pairs = [
         (spts_hbm, spts), (spot_hbm, spot), (src_hbm.at[0], row_src), (tgt_hbm.at[0], row_tgt),
         (src_hbm.at[0], ids_src), (tgt_hbm.at[0], ids_tgt), (count_hbm, count_ref),
         (slogw_hbm, slogw), (tlogw_hbm, tlogw),
     ]
     small = [pltpu.make_async_copy(a, b, load_sem.at[k]) for k, (a, b) in enumerate(pairs)]
-    for load in small:
+    for load in small[0:2]:
+        load.start()
+    for peer in peers[nx:]:
+        greet(peer)
+    for load in small[2:]:
         load.start()
     width = n_tb * BLOCK // CHUNKS
     loads = []
@@ -157,12 +174,7 @@
             device_id=where, device_id_type=MESH,
         )
 
-    def chip(d):
-        return (me_s, lax.rem(my_x + d, nx) * 2 + my_c)
-
-    other_core = (me_s, my_x * 2 + 1 - my_c)
     mine = xbuf.at[me_t]
-    order = sorted(range(1, nx), key=lambda d: -min(d, nx - d))
     sent = [remote(mine, mine, gather_send.at[d], gather_recv.at[me_t], chip(d)) for d in order]
     sent.append(remote(mine, mine, gather_send.at[0], gather_recv.at[me_t], other_core))
     for copy in sent:
@@ -247,7 +259,7 @@
             far[pl.ds(p, 1), :] = jnp.where(n_tb + p < count, row, LOWEST)
         return carry
 
-    lax.fori_loop(0, n_extra // UNROLL, far_columns, 0)
+    repeat(n_extra // UNROLL, far_columns, 0)
 
     def band(y):
         return pl.ds(pl.multiple_of(y * per_y, per_y), per_y)
@@ -268,14 +280,9 @@
             if not (isinstance(d, int) and d == 0):
                 to_y(d).start()
 
-    def near_pair(m, carry):
+    extra[...] = owner_steps(far[...], pick_t, gather_t)
+    for m in range(ny // 2 - 1):
         near_columns([ny // 2 - m, ny // 2 + 1 + m])
-        return carry
-
-    extra[...] = owner_steps(far[...], pick_t, gather_t)
-    if ny > 2:
-        near_columns([ny // 2, ny // 2 + 1])
-        lax.fori_loop(1, ny // 2 - 1, near_pair, 0)
     near_columns([1])
     near_columns([0])
     recv_y[my_y] = part[band(my_y), :]
@@ -309,7 +316,7 @@
 
     line = lax.broadcasted_iota(jnp.int32, (16, BLOCK), 0)
 
-    def near_rows(ds):
+    def near_rows(ds, top):
         bands = [lax.rem(my_y + d, ny) for d in ds]
         values = []
         for y, d in zip(bands, ds):
@@ -336,32 +343,28 @@
                 both = [r[:48], high.astype(bf16), r[64:112], low.astype(bf16)]
                 turned = jnp.concatenate(both, axis=0).T
                 a_tgt[b] = turned
-                lse[pl.ds(b, 1), :] = column_lse(turned, r_src[row_ids[0, b]])
-
-    def near_row_pair(m, carry):
-        near_rows([m, ny - m])
-        return carry
-
-    near_rows([0])
-    lax.fori_loop(1, ny // 2, near_row_pair, 0)
-    near_rows([ny // 2])
-
-    def far_rows(k, carry):
+                row = column_lse(turned, r_src[row_ids[0, b]])
+                lse[pl.ds(b, 1), :] = row
+                top = raise_peaks(top, [row], [row_ids[0, b]])
+        return top
+
+    row_peak = near_rows([0], jnp.full((n_sb, BLOCK), LOWEST, f32))
+    arrivals = sorted(range(1, ny), key=lambda d: min(d, ny - d))
+    for group in (arrivals[0:2], arrivals[2:6], arrivals[6:]):
+        if group:
+            row_peak = near_rows(group, row_peak)
+
+    def far_rows(k, top):
         for step in range(UNROLL):
             p = k * UNROLL + step
-            row = column_lse(a_tgt[ids_tgt[0, n_tb + p]], r_src[ids_src[0, n_tb + p]])
-            far[pl.ds(p, 1), :] = jnp.where(n_tb + p < count, row, LOWEST)
-        return carry
-
-    lax.fori_loop(0, n_extra // UNROLL, far_rows, 0)
-    def lift(part, first, k, top):
-        at = [k * 8 + step for step in range(8)]
-        ids = [row_ids[0, first + p] for p in at]
-        return raise_peaks(top, [part[pl.ds(p, 1), :] for p in at], ids)
-
-    row_peak = jnp.full((n_sb, BLOCK), LOWEST, f32)
-    row_peak = lax.fori_loop(0, n_tb // 8, functools.partial(lift, lse, 0), row_peak)
-    row_peak = lax.fori_loop(0, n_extra // 8, functools.partial(lift, far, n_tb), row_peak)
+            owner = ids_src[0, n_tb + p]
+            row = column_lse(a_tgt[ids_tgt[0, n_tb + p]], r_src[owner])
+            row = jnp.where(n_tb + p < count, row, LOWEST)
+            far[pl.ds(p, 1), :] = row
+            top = raise_peaks(top, [row], [owner])
+        return top
+
+    row_peak = repeat(n_extra // UNROLL, far_rows, row_peak)
     both = jnp.concatenate([lse[...], far[...]], axis=0)
     rowpart[...] = owner_sums(row_peak, both, pick_s, gather_s)
 
@@ -379,14 +382,14 @@
         ],
         axis=0,
     )
-    collect(nt, me_t, along_t, lambda t: recv_x.at[t], x_send, x_recv)
-    out_s[...] = potential + 0.5 * slogw[...] - (0.5 * LN2) * merge(recv_x[...])
-
+    rest = potential + 0.5 * slogw[...]
     for copy in sent + relays:
         copy.wait_send()
     for n, to in ((ny, to_y), (nz, to_z), (ny, to_all), (nt, to_t)):
         for d in range(1, n):
             to(d).wait_send()
+    collect(nt, me_t, along_t, lambda t: recv_x.at[t], x_send, x_recv)
+    out_s[...] = rest - (0.5 * LN2) * merge(recv_x[...])
 
 
 def local(

time: 50.1 us -> 49.4 us (0.986)
  Pallas kernels: 47.5 us -> 46.7 us
    pallas_call x1, Pallas kernels: 47.5 us -> 46.7 us  [local(): pl.pallas_call(functools.partial(kernel, (ny, nz, nt, n_tb, n_sb, slots,...]
where the time goes in v4:
time: 49.4 us; the launch traced here: 49.2 us
  Pallas kernels  46.7 us (95%)
  between operations  1.29 us (3%)
  local copies, waits for them, and re-layouts  1.23 us (2%)
    pallas_call x1, Pallas kernels, local(): pl.pallas_call(functools.partial(kernel, (ny, nz, nt, n_tb, n_sb, slots,...  46.7 us
    unnamed x2, local copies, waits for them, and re-layouts  1.23 us

profile of v4, /device:TPU:1, one launch (start us, length us, event | category | flops | bytes accessed | tf_op | source)
XLA Modules:
  0.0 49.2 jit_solution(527245729431737289)
XLA Ops:
  1.3 46.7 %shard_map.95 = (f32[128,128]{1,0:T(8,128)S(1)}, f32[16,128]{1,0:T(8,128)S(1)}) custom-call(f32[50,256]{1,0:T(8,128)} %spts_hbm.1, f32[1,256]{1,0:T(1,128)} %bitcast.9, f32[16,128]{1,0:T(8,128)} %bitcast.8, f32[50,16384]{1,0:T(8,128)} %tpts_hbm.1, f32[128,128]{1,0:T(8,128)} %bitcast.7, s32[1,1,256]{2,1,0:T(1,128)} %src_hbm.1, s32[1,1,256]{2,1,0:T(1,128)} %tgt_hbm.1, ...), custom_call_target="tpu_custom_call" | custom-call | tf_op jit(solution)/shard_map/pallas_call | solution.py:418
  48.0 0.6 %copy.12 = f32[16384]{0:T(1024)} copy(f32[16384]{0:T(1024)S(1)} %bitcast.5) | data formatting | bytes 131072
  48.6 0.6 %copy.13 = f32[2048]{0:T(1024)} copy(f32[2048]{0:T(1024)S(1)} %bitcast.6) | data formatting | bytes 16384

commit v5 on v4

--- a/solution.py
+++ b/solution.py
@@ -129,8 +129,8 @@
         [chip(d) for d in order]
         + [other_core]
         + [(me_s, lax.rem(my_x + d, nx) * 2 + 1 - my_c) for d in order]
-        + [along_y(d) for d in range(1, ny)]
-        + [along_z(d) for d in range(1, nz)]
+        + [along_y(d) for d in sorted(range(1, ny), key=lambda d: -min(d, ny - d))]
+        + [along_z(d) for d in sorted(range(1, nz), key=lambda d: -min(d, nz - d))]
     )
     def greet(peer):
         pl.semaphore_signal(barrier, inc=1, device_id=peer, device_id_type=MESH)
@@ -237,19 +237,29 @@
             r_src[b] = both
             a_src[b] = both.T
 
-    source(me_t)
-    relays = []
-    for d in reversed(order):
+    def pass_on(d):
         t = lax.rem(my_x + d, nx) * 2 + my_c
         arrived(xbuf.at[t], gather_recv.at[t], chip(d))
         relay = remote(xbuf.at[t], xbuf.at[t], relay_send.at[d], gather_recv.at[t], other_core)
         relay.start()
-        relays.append(relay)
-        source(t)
-    for d in [0] + order[::-1]:
+        return relay
+
+    def from_other(d):
         t = lax.rem(my_x + d, nx) * 2 + 1 - my_c
         arrived(xbuf.at[t], gather_recv.at[t], other_core)
         source(t)
+
+    source(me_t)
+    from_other(0)
+    near_first = order[::-1]
+    relays = [pass_on(d) for d in near_first[:-1]]
+    for d in near_first[:-1]:
+        source(lax.rem(my_x + d, nx) * 2 + my_c)
+    relays.append(pass_on(near_first[-1]))
+    for d in near_first[:-1]:
+        from_other(d)
+    source(lax.rem(my_x + near_first[-1], nx) * 2 + my_c)
+    from_other(near_first[-1])
     base_copy.wait()
 
     def far_columns(k, carry):

time: 49.4 us -> 49 us (level)
  no operation moved by 1% of the time
where the time goes in v5:
time: 49 us; the launch traced here: 48.8 us
  Pallas kernels  46.3 us (94%)
  between operations  1.29 us (3%)
  local copies, waits for them, and re-layouts  1.23 us (3%)
    pallas_call x1, Pallas kernels, local(): pl.pallas_call(functools.partial(kernel, (ny, nz, nt, n_tb, n_sb, slots,...  46.3 us
    unnamed x2, local copies, waits for them, and re-layouts  1.23 us

profile of v5, /device:TPU:1, one launch (start us, length us, event | category | flops | bytes accessed | tf_op | source)
XLA Modules:
  0.0 48.8 jit_solution(13289767654109005063)
XLA Ops:
  1.3 46.3 %shard_map.95 = (f32[128,128]{1,0:T(8,128)S(1)}, f32[16,128]{1,0:T(8,128)S(1)}) custom-call(f32[50,256]{1,0:T(8,128)} %spts_hbm.1, f32[1,256]{1,0:T(1,128)} %bitcast.9, f32[16,128]{1,0:T(8,128)} %bitcast.8, f32[50,16384]{1,0:T(8,128)} %tpts_hbm.1, f32[128,128]{1,0:T(8,128)} %bitcast.7, s32[1,1,256]{2,1,0:T(1,128)} %src_hbm.1, s32[1,1,256]{2,1,0:T(1,128)} %tgt_hbm.1, ...), custom_call_target="tpu_custom_call" | custom-call | tf_op jit(solution)/shard_map/pallas_call | solution.py:428
  47.6 0.6 %copy.12 = f32[16384]{0:T(1024)} copy(f32[16384]{0:T(1024)S(1)} %bitcast.5) | data formatting | bytes 131072
  48.2 0.6 %copy.13 = f32[2048]{0:T(1024)} copy(f32[2048]{0:T(1024)S(1)} %bitcast.6) | data formatting | bytes 16384

commit v6 on v5

--- a/solution.py
+++ b/solution.py
@@ -338,7 +338,6 @@
             rows = band(y)
             total = full[rows, :]
             weight = tlogw[rows, :]
-            out_t[rows, :] = 0.5 * weight - (0.5 * LN2) * (total - y_sq[rows, :])
             v = LOG2E * weight - total
             high, low = split(v)
             values.append((high.astype(f32), low.astype(f32), residue(v)))
@@ -393,6 +392,7 @@
         axis=0,
     )
     rest = potential + 0.5 * slogw[...]
+    out_t[...] = 0.5 * tlogw[...] - (0.5 * LN2) * (full[...] - y_sq[...])
     for copy in sent + relays:
         copy.wait_send()
     for n, to in ((ny, to_y), (nz, to_z), (ny, to_all), (nt, to_t)):

time: 49 us -> 49 us (level)
  no operation moved by 1% of the time
where the time goes in v6:
time: 49 us; the launch traced here: 48.8 us
  Pallas kernels  46.3 us (94%)
  between operations  1.29 us (3%)
  local copies, waits for them, and re-layouts  1.23 us (3%)
    pallas_call x1, Pallas kernels, local(): pl.pallas_call(functools.partial(kernel, (ny, nz, nt, n_tb, n_sb, slots,...  46.3 us
    unnamed x2, local copies, waits for them, and re-layouts  1.23 us

profile of v6, /device:TPU:1, one launch (start us, length us, event | category | flops | bytes accessed | tf_op | source)
XLA Modules:
  0.0 48.8 jit_solution(4359785117175021037)
XLA Ops:
  1.3 46.3 %shard_map.95 = (f32[128,128]{1,0:T(8,128)S(1)}, f32[16,128]{1,0:T(8,128)S(1)}) custom-call(f32[50,256]{1,0:T(8,128)} %spts_hbm.1, f32[1,256]{1,0:T(1,128)} %bitcast.9, f32[16,128]{1,0:T(8,128)} %bitcast.8, f32[50,16384]{1,0:T(8,128)} %tpts_hbm.1, f32[128,128]{1,0:T(8,128)} %bitcast.7, s32[1,1,256]{2,1,0:T(1,128)} %src_hbm.1, s32[1,1,256]{2,1,0:T(1,128)} %tgt_hbm.1, ...), custom_call_target="tpu_custom_call" | custom-call | tf_op jit(solution)/shard_map/pallas_call | solution.py:428
  47.6 0.6 %copy.12 = f32[16384]{0:T(1024)} copy(f32[16384]{0:T(1024)S(1)} %bitcast.5) | data formatting | bytes 131072
  48.2 0.6 %copy.13 = f32[2048]{0:T(1024)} copy(f32[2048]{0:T(1024)S(1)} %bitcast.6) | data formatting | bytes 16384
